TPU v7x, 32 devices: a whole 2x2x4 slice. The times are simulated.
32 devices in a mesh: group: 2 (over x), head: 16 (over z, y, core).
Axes of the slice: x: 2, y: 2, z: 4, core: 2. Of those that a mesh axis runs over, the one named last changes fastest.
Arguments:
- queries: bfloat16 [4096, 64, 192], P(('group', 'head')), parts along dimension 0, may hold values from -20 to 20
- latent: bfloat16 [4096, 512], P(('group', 'head')), parts along dimension 0, may hold values from -6 to 6
- rope_key: bfloat16 [4096, 64], P(('group', 'head')), parts along dimension 0, may hold values from -8 to 8
- key_up: bfloat16 [512, 64, 128], P(None, 'head'), may hold values from -0.25 to 0.25
- value_up: bfloat16 [512, 64, 128], P(None, 'head'), may hold values from -0.25 to 0.25
- first_key: int32 [4096], P('group'), parts along dimension 0, may hold values from 0 to 2047, as said below
- out_grad: bfloat16 [4096, 64, 128], P(('group', 'head')), parts along dimension 0, may hold values from -6 to 6
Outputs:
- query_grad: bfloat16 [4096, 64, 192], P(('group', 'head')), parts along dimension 0
- latent_grad: bfloat16 [4096, 512], P(('group', 'head')), parts along dimension 0
- rope_key_grad: bfloat16 [4096, 64], P(('group', 'head')), parts along dimension 0
- key_up_grad: float32 [1024, 64, 128], P('group', 'head'), parts along dimension 0
- value_up_grad: float32 [1024, 64, 128], P('group', 'head'), parts along dimension 0
There are 2 independent parts, one for each index of `group`. A program takes and returns all parts, laid end to end along the dimension named above; an argument that names none is the same for every part. Nothing has to cross between parts.
Inputs may be any that keep to these rules, and one draw needn't show every extreme that they name: first_key never decreases as i grows, first_key[i] <= i, and i - first_key[i] < 512.
All inputs are finite; a program needn't handle non-finite values.
Results may differ from a plain program's by a relative error of at most 0.024.
Values may be sent and summed in bfloat16 or wider, within the bound.
A program may use at most 128 MiB of HBM per device.

v0:
```python
import math

import jax
import jax.numpy as jnp
from jax import lax
from jax.sharding import PartitionSpec as P


def expand(latent_all, key_up, value_up):
    key_nope = jnp.einsum(
        "tc,chd->thd", latent_all, key_up, preferred_element_type=jnp.float32
    ).astype(jnp.bfloat16)
    values = jnp.einsum(
        "tc,chd->thd", latent_all, value_up, preferred_element_type=jnp.float32
    ).astype(jnp.bfloat16)
    return (key_nope, values)


def shards(queries, latent, rope_key, key_up, value_up, first_key, out_grad):
    wide = jnp.float32
    low = jnp.bfloat16
    own_rows = queries.shape[0]
    devices = lax.axis_size("head")
    seq_len = own_rows * devices
    local_heads = key_up.shape[1]
    nope_width = key_up.shape[2]
    qk_width = queries.shape[2]
    value_width = out_grad.shape[2]
    score_scale = 1.0 / math.sqrt(qk_width)
    query_all, grad_all = (
        lax.all_to_all(queries, "head", split_axis=1, concat_axis=0, tiled=True),
        lax.all_to_all(out_grad, "head", split_axis=1, concat_axis=0, tiled=True),
    )
    latent_all, rope_all = (
        lax.all_gather(latent, "head", axis=0, tiled=True),
        lax.all_gather(rope_key, "head", axis=0, tiled=True),
    )
    key_nope, values = expand(latent_all, key_up, value_up)
    keys_all = jnp.concatenate(
        [
            key_nope,
            jnp.broadcast_to(rope_all[:, None, :], (seq_len, local_heads, rope_all.shape[1])),
        ],
        axis=2,
    )
    query_rows = 4 * own_rows
    reach = 4 * own_rows
    window = query_rows + reach
    block_count = seq_len // query_rows

    def backward_block(block_index, carry):
        query_grad, key_grad, value_grad = carry
        first_row = block_index * query_rows
        first_col = jnp.maximum(first_row - reach, 0)
        query_block = lax.dynamic_slice_in_dim(query_all, first_row, query_rows, 0)
        grad_block = lax.dynamic_slice_in_dim(grad_all, first_row, query_rows, 0)
        key_block = lax.dynamic_slice_in_dim(keys_all, first_col, window, 0)
        value_block = lax.dynamic_slice_in_dim(values, first_col, window, 0)
        limits = lax.dynamic_slice_in_dim(first_key, first_row, query_rows, 0)
        row_pos = first_row + jnp.arange(query_rows, dtype=jnp.int32)
        col_pos = first_col + jnp.arange(window, dtype=jnp.int32)
        visible = (col_pos[None, :] >= limits[:, None]) & (col_pos[None, :] <= row_pos[:, None])
        scores = (
            jnp.einsum("ihd,jhd->hij", query_block, key_block, preferred_element_type=wide)
            * score_scale
        )
        scores = jnp.where(visible[None], scores, -jnp.inf)
        peak = jnp.max(scores, axis=2, keepdims=True)
        log_total = peak + jnp.log(jnp.sum(jnp.exp(scores - peak), axis=2, keepdims=True))
        probs = jnp.exp(scores - log_total)
        probs_low = probs.astype(low)
        attended = jnp.einsum("hij,jhd->ihd", probs_low, value_block, preferred_element_type=wide)
        delta = jnp.sum(grad_block.astype(wide) * attended, axis=2).T[:, :, None]
        prob_grad = jnp.einsum("ihd,jhd->hij", grad_block, value_block, preferred_element_type=wide)
        score_grad = (probs * (prob_grad - delta)).astype(low)
        block_qgrad = (
            score_scale
            * jnp.einsum("hij,jhd->ihd", score_grad, key_block, preferred_element_type=wide)
        ).astype(low)
        block_kgrad = score_scale * jnp.einsum(
            "hij,ihd->jhd", score_grad, query_block, preferred_element_type=wide
        )
        block_vgrad = jnp.einsum("hij,ihd->jhd", probs_low, grad_block, preferred_element_type=wide)
        query_grad = lax.dynamic_update_slice_in_dim(query_grad, block_qgrad, first_row, 0)
        key_grad = lax.dynamic_update_slice_in_dim(
            key_grad,
            lax.dynamic_slice_in_dim(key_grad, first_col, window, 0) + block_kgrad,
            first_col,
            0,
        )
        value_grad = lax.dynamic_update_slice_in_dim(
            value_grad,
            lax.dynamic_slice_in_dim(value_grad, first_col, window, 0) + block_vgrad,
            first_col,
            0,
        )
        return (query_grad, key_grad, value_grad)

    start = (
        jnp.zeros((seq_len, local_heads, qk_width), low),
        jnp.zeros((seq_len, local_heads, qk_width), wide),
        jnp.zeros((seq_len, local_heads, value_width), wide),
    )
    query_grad, key_grad, value_grad = lax.fori_loop(0, block_count, backward_block, start)
    key_low = key_grad.astype(low)
    value_low = value_grad.astype(low)
    key_part = key_low[:, :, :nope_width]
    key_up_grad = jnp.einsum("tc,thd->chd", latent_all, key_part, preferred_element_type=wide)
    value_up_grad = jnp.einsum("tc,thd->chd", latent_all, value_low, preferred_element_type=wide)
    query_out = lax.all_to_all(query_grad, "head", split_axis=0, concat_axis=1, tiled=True)
    latent_part = jnp.einsum(
        "thd,chd->tc", key_part, key_up, preferred_element_type=wide
    ) + jnp.einsum("thd,chd->tc", value_low, value_up, preferred_element_type=wide)
    rope_part = jnp.sum(key_low[:, :, nope_width:].astype(wide), axis=1)
    latent_sum, rope_sum = (
        lax.psum_scatter(
            latent_part.astype(jnp.bfloat16), "head", scatter_dimension=0, tiled=True
        ).astype(jnp.float32),
        lax.psum_scatter(
            rope_part.astype(jnp.bfloat16), "head", scatter_dimension=0, tiled=True
        ).astype(jnp.float32),
    )
    return (query_out, latent_sum.astype(low), rope_sum.astype(low), key_up_grad, value_up_grad)


def solution(mesh):
    return jax.shard_map(
        shards,
        mesh=mesh,
        in_specs=(
            P(("group", "head"), None, None),
            P(("group", "head"), None),
            P(("group", "head"), None),
            P(None, "head", None),
            P(None, "head", None),
            P("group"),
            P(("group", "head"), None, None),
        ),
        out_specs=(
            P(("group", "head"), None, None),
            P(("group", "head"), None),
            P(("group", "head"), None),
            P("group", "head", None),
            P("group", "head", None),
        ),
        check_vma=False,
    )
```

profile of v0, /device:TPU:31, one launch (start us, length us, event | category | flops | bytes accessed | tf_op | source)
XLA Modules:
  0.0 611.9 jit_solution(4153530364047778592)
XLA Ops:
  10.2 52.7 %all_to_all.54 = bf16[128,64,128]{2,0,1:T(8,128)(2,1)S(1)} all-to-all(bf16[128,64,128]{2,0,1:T(8,128)(2,1)S(1)} %copy.32), channel_id=1, replica_groups=mesh['group'=2,'head'=16] {'head'}, dimensions={1} | all-to-all | bytes 4194304 | tf_op jit(solution)/shard_map/all_to_all | solution.py:32
  62.9 6.0 all-to-all-start
  71.0 89.8 %all_gather.7 = bf16[2048,64]{0,1:T(8,128)(2,1)S(1)} all-gather(bf16[128,64]{0,1:T(8,128)(2,1)S(1)} %copy-done.10), channel_id=1, replica_groups=mesh['group'=2,'head'=16] {'head'}, dimensions={0}, use_global_device_ids=true | all-gather | bytes 278528 | tf_op jit(solution)/shard_map/all_gather | solution.py:36
  170.2 5.6 copy.57
  175.8 5.8 all_to_all.42
  189.5 250.4 %while.19 = (s32[]{:T(128)}, bf16[2048,4,192]{0,2,1:T(8,128)(2,1)}, f32[2048,4,192]{0,2,1:T(8,128)}, f32[2048,4,128]{0,2,1:T(8,128)}, bf16[2048,4,192]{0,2,1:T(8...) while((s32[]{:T(128)}, bf16[2048,4,192]{0,2,1:T(8,128)(2,1)}, ...), condition=%wide.region_4.5_spmd, body=%wide.region_0.4_spmd.sunk | while | flops 4075812352 | bytes 215853504 | solution.py:104
  204.0 10.4 %dynamic_update_slice.36 = f32[2048,4,128]{0,2,1:T(8,128)} dynamic-update-slice(f32[2048,4,128]{0,2,1:T(8,128)} %get-tuple-element.336, f32[1024,4,128]{0,2,1:T(8,128)S(1)} %bitcast_add_fusion.6, s32[]{:T(128)S(6)} %max.11, s32[]{:T(128)} %constant.80.clone.1..sunk, s32[]{:T(128)} %constant.80.clone.1..sunk) | dynamic-update-slice | bytes 4194308 | tf_op jit(solution)/shard_map/while/body/eval_jaxpr/dynamic_update_slice | solution.py:91
  214.4 6.3 %fusion.78 = f32[512,4]{0,1:T(4,128)S(1)} fusion(bf16[2048,4,128]{2,0,1:T(8,128)(2,1)} %get-tuple-element.355, s32[]{:T(128)S(6)} %max.11, bf16[2048,4,128]{2,0,1:T(8,128)(2,1)} %get-tuple-element.354, s32[]{:T(128)S(6)} %select_n.54, f32[4,512,1024]{2,1,0:T(8,128)} %copy-done.2, f32[4,512]{1,0:T(4,128)S(1)} %log_add_fusion.2, ...), kind=kOutput, calls=%fused_computation.17.clone.1 | convolution fusion | flops 546043904 | bytes 10502152 | tf_op jit(solution)/shard_map/while/body/eval_jaxpr/hij,jhd->ihd/dot_general | solution.py:72
  231.9 15.7 %dynamic_update_slice.35 = f32[2048,4,192]{0,2,1:T(8,128)} dynamic-update-slice(f32[2048,4,192]{0,2,1:T(8,128)} %get-tuple-element.335, f32[1024,4,192]{0,2,1:T(8,128)} %bitcast_add_fusion.5, s32[]{:T(128)S(6)} %max.11, s32[]{:T(128)} %constant.80.clone.1..sunk, s32[]{:T(128)} %constant.80.clone.1..sunk) | dynamic-update-slice | bytes 6291460 | tf_op jit(solution)/shard_map/while/body/eval_jaxpr/dynamic_update_slice | solution.py:85
  247.5 5.2 fusion.79
  267.2 10.4 %dynamic_update_slice.36 = f32[2048,4,128]{0,2,1:T(8,128)} dynamic-update-slice(f32[2048,4,128]{0,2,1:T(8,128)} %get-tuple-element.336, f32[1024,4,128]{0,2,1:T(8,128)S(1)} %bitcast_add_fusion.6, s32[]{:T(128)S(6)} %max.11, s32[]{:T(128)} %constant.80.clone.1..sunk, s32[]{:T(128)} %constant.80.clone.1..sunk) | dynamic-update-slice | bytes 4194308 | tf_op jit(solution)/shard_map/while/body/eval_jaxpr/dynamic_update_slice | solution.py:91
  277.5 6.3 %fusion.78 = f32[512,4]{0,1:T(4,128)S(1)} fusion(bf16[2048,4,128]{2,0,1:T(8,128)(2,1)} %get-tuple-element.355, s32[]{:T(128)S(6)} %max.11, bf16[2048,4,128]{2,0,1:T(8,128)(2,1)} %get-tuple-element.354, s32[]{:T(128)S(6)} %select_n.54, f32[4,512,1024]{2,1,0:T(8,128)} %copy-done.2, f32[4,512]{1,0:T(4,128)S(1)} %log_add_fusion.2, ...), kind=kOutput, calls=%fused_computation.17.clone.1 | convolution fusion | flops 546043904 | bytes 10502152 | tf_op jit(solution)/shard_map/while/body/eval_jaxpr/hij,jhd->ihd/dot_general | solution.py:72
  284.3 4.5 multiply_convert_fusion.3
  295.0 15.7 %dynamic_update_slice.35 = f32[2048,4,192]{0,2,1:T(8,128)} dynamic-update-slice(f32[2048,4,192]{0,2,1:T(8,128)} %get-tuple-element.335, f32[1024,4,192]{0,2,1:T(8,128)} %bitcast_add_fusion.5, s32[]{:T(128)S(6)} %max.11, s32[]{:T(128)} %constant.80.clone.1..sunk, s32[]{:T(128)} %constant.80.clone.1..sunk) | dynamic-update-slice | bytes 6291460 | tf_op jit(solution)/shard_map/while/body/eval_jaxpr/dynamic_update_slice | solution.py:85
  310.7 5.2 fusion.79
  330.3 10.1 %dynamic_update_slice.36 = f32[2048,4,128]{0,2,1:T(8,128)} dynamic-update-slice(f32[2048,4,128]{0,2,1:T(8,128)} %get-tuple-element.336, f32[1024,4,128]{0,2,1:T(8,128)S(1)} %bitcast_add_fusion.6, s32[]{:T(128)S(6)} %max.11, s32[]{:T(128)} %constant.80.clone.1..sunk, s32[]{:T(128)} %constant.80.clone.1..sunk) | dynamic-update-slice | bytes 4194308 | tf_op jit(solution)/shard_map/while/body/eval_jaxpr/dynamic_update_slice | solution.py:91
  340.4 6.3 %fusion.78 = f32[512,4]{0,1:T(4,128)S(1)} fusion(bf16[2048,4,128]{2,0,1:T(8,128)(2,1)} %get-tuple-element.355, s32[]{:T(128)S(6)} %max.11, bf16[2048,4,128]{2,0,1:T(8,128)(2,1)} %get-tuple-element.354, s32[]{:T(128)S(6)} %select_n.54, f32[4,512,1024]{2,1,0:T(8,128)} %copy-done.2, f32[4,512]{1,0:T(4,128)S(1)} %log_add_fusion.2, ...), kind=kOutput, calls=%fused_computation.17.clone.1 | convolution fusion | flops 546043904 | bytes 10502152 | tf_op jit(solution)/shard_map/while/body/eval_jaxpr/hij,jhd->ihd/dot_general | solution.py:72
  347.2 4.5 multiply_convert_fusion.3
  357.9 15.5 %dynamic_update_slice.35 = f32[2048,4,192]{0,2,1:T(8,128)} dynamic-update-slice(f32[2048,4,192]{0,2,1:T(8,128)} %get-tuple-element.335, f32[1024,4,192]{0,2,1:T(8,128)} %bitcast_add_fusion.5, s32[]{:T(128)S(6)} %max.11, s32[]{:T(128)} %constant.80.clone.1..sunk, s32[]{:T(128)} %constant.80.clone.1..sunk) | dynamic-update-slice | bytes 6291460 | tf_op jit(solution)/shard_map/while/body/eval_jaxpr/dynamic_update_slice | solution.py:85
  373.4 5.2 fusion.79
  393.0 9.5 %dynamic_update_slice.36 = f32[2048,4,128]{0,2,1:T(8,128)} dynamic-update-slice(f32[2048,4,128]{0,2,1:T(8,128)} %get-tuple-element.336, f32[1024,4,128]{0,2,1:T(8,128)S(1)} %bitcast_add_fusion.6, s32[]{:T(128)S(6)} %max.11, s32[]{:T(128)} %constant.80.clone.1..sunk, s32[]{:T(128)} %constant.80.clone.1..sunk) | dynamic-update-slice | bytes 4194308 | tf_op jit(solution)/shard_map/while/body/eval_jaxpr/dynamic_update_slice | solution.py:91
  402.4 6.3 %fusion.78 = f32[512,4]{0,1:T(4,128)S(1)} fusion(bf16[2048,4,128]{2,0,1:T(8,128)(2,1)} %get-tuple-element.355, s32[]{:T(128)S(6)} %max.11, bf16[2048,4,128]{2,0,1:T(8,128)(2,1)} %get-tuple-element.354, s32[]{:T(128)S(6)} %select_n.54, f32[4,512,1024]{2,1,0:T(8,128)} %copy-done.2, f32[4,512]{1,0:T(4,128)S(1)} %log_add_fusion.2, ...), kind=kOutput, calls=%fused_computation.17.clone.1 | convolution fusion | flops 546043904 | bytes 10502152 | tf_op jit(solution)/shard_map/while/body/eval_jaxpr/hij,jhd->ihd/dot_general | solution.py:72
  409.3 4.5 multiply_convert_fusion.3
  419.9 14.9 %dynamic_update_slice.35 = f32[2048,4,192]{0,2,1:T(8,128)} dynamic-update-slice(f32[2048,4,192]{0,2,1:T(8,128)} %get-tuple-element.335, f32[1024,4,192]{0,2,1:T(8,128)} %bitcast_add_fusion.5, s32[]{:T(128)S(6)} %max.11, s32[]{:T(128)} %constant.80.clone.1..sunk, s32[]{:T(128)} %constant.80.clone.1..sunk) | dynamic-update-slice | bytes 6291460 | tf_op jit(solution)/shard_map/while/body/eval_jaxpr/dynamic_update_slice | solution.py:85
  434.8 5.1 fusion.79
  439.9 7.2 %copy.35 = bf16[2048,4,192]{2,1,0:T(4,128)(2,1)} copy(bf16[2048,4,192]{0,2,1:T(8,128)(2,1)} %get-tuple-element.227) | data formatting | bytes 6291456 | tf_op jit(solution)/shard_map/while | solution.py:104
  447.1 6.0 all-to-all-start.2
  453.1 6.7 %copy.37 = bf16[2048,4,192]{2,0,1:T(8,128)(2,1)} copy(f32[2048,4,192]{0,2,1:T(8,128)} %get-tuple-element.228) | data formatting | bytes 9437184 | tf_op jit(solution)/shard_map/while | solution.py:104
  482.0 58.4 %reduce-scatter.7.cloned.1.call-done = bf16[128,64]{1,0:T(8,128)(2,1)} async-done(((bf16[2048,64]{1,0:T(8,128)(2,1)}), bf16[128,64]{1,0:T(8,128)(2,1)}) %reduce-scatter.7.cloned.1.call-update) | async-done | bytes 16400
  541.8 6.1 %all-to-all-done.2 = bf16[2048,4,192]{2,1,0:T(4,128)(2,1)} async-done(((bf16[2048,4,192]{2,1,0:T(4,128)(2,1)}), bf16[2048,4,192]{2,1,0:T(4,128)(2,1)}, u32[]{:S(2)}, u32[]{:S(2)}) %all-to-all-start.2) | async-done | bytes 3145760 | tf_op jit(solution)/shard_map/all_to_all | solution.py:110
  548.0 7.2 %copy.36 = bf16[128,16,4,192]{0,3,2,1:T(8,128)(2,1)} copy(bf16[128,16,4,192]{3,2,0,1:T(4,128)(2,1)} %bitcast.14) | data formatting | bytes 6291456 | tf_op jit(solution)/shard_map/all_to_all | solution.py:110
  555.1 50.2 %reduce-scatter.5.cloned.1.call-done = bf16[128,512]{1,0:T(8,128)(2,1)} async-done(((bf16[2048,512]{1,0:T(8,128)(2,1)}), bf16[128,512]{1,0:T(8,128)(2,1)}) %reduce-scatter.5.cloned.1.call-update) | async-done | bytes 131088 | tf_op jit(solution)/shard_map/reduce_scatter | solution.py:116
  (138 shorter events, 135.0 us)
Async XLA Ops:
  7.2 160.2 %copy-start = (bf16[512,4,128]{2,1,0:T(4,128)(2,1)S(1)}, bf16[512,4,128]{2,1,0:T(4,128)(2,1)}, u32[]{:S(2)}) copy-start(bf16[512,4,128]{2,1,0:T(4,128)(2,1)} %param.13) | copy-start | bytes 1572868
  62.9 8.1 %copy-start.10 = (bf16[128,64]{0,1:T(8,128)(2,1)S(1)}, bf16[128,64]{0,1:T(8,128)(2,1)}, u32[]{:S(2)}) copy-start(bf16[128,64]{0,1:T(8,128)(2,1)} %param.11) | copy-start | bytes 49156
  62.9 107.3 %all-to-all-start = ((bf16[128,64,192]{0,2,1:T(8,128)(2,1)}), bf16[128,64,192]{0,2,1:T(8,128)(2,1)}, u32[]{:S(2)}, u32[]{:S(2)}) async-start(bf16[128,64,192]{0,2,1:T(8,128)(2,1)} %param.9), calls=%async_computation | async-start | bytes 6291456 | tf_op jit(solution)/shard_map/all_to_all | solution.py:31
  68.9 91.8 %all-gather.2.cloned.1.call-start = ((), (), s32[]{:S(2)}) async-start(), calls=%async_computation.5 | async-start | bytes 2228224 | tf_op jit(solution)/shard_map/all_gather | solution.py:35
  70.9 92.7 %copy-start.8 = (bf16[512,4,128]{0,2,1:T(8,128)(2,1)}, bf16[512,4,128]{0,2,1:T(8,128)(2,1)S(1)}, u32[]{:S(2)}) copy-start(bf16[512,4,128]{0,2,1:T(8,128)(2,1)S(1)} %copy.30) | copy-start | bytes 1572868
  195.0 4.3 copy-start.2
  195.0 5.2 copy-start.4
  214.4 6.3 %copy-start.3 = (f32[4,512,1024]{2,1,0:T(8,128)S(1)}, f32[4,512,1024]{2,1,0:T(8,128)}, u32[]{:S(2)}) copy-start(f32[4,512,1024]{2,1,0:T(8,128)} %copy-done.2) | copy-start | bytes 25165828 | tf_op jit(solution)/shard_map/while
  214.4 6.8 %copy-start.11 = (bf16[2048,4,128]{2,0,1:T(8,128)(2,1)S(1)}, bf16[2048,4,128]{2,0,1:T(8,128)(2,1)}, u32[]{:S(2)}) copy-start(bf16[2048,4,128]{2,0,1:T(8,128)(2,1)} %get-tuple-element.355) | copy-start | bytes 6291460 | tf_op jit(solution)/shard_map/while
  214.4 13.3 %slice-start = ((s8[6291456]{0:T(1024)(128)(4,1)}), s8[4194304]{0:T(1024)(128)(4,1)S(1)}, s32[]{:S(2)}) async-start(s8[6291456]{0:T(1024)(128)(4,1)} %bitcast.74), calls=%async_computation.8 | async-start | bytes 8388608 | tf_op jit(solution)/shard_map/while
  221.2 6.5 %slice-start.1 = ((s8[6291456]{0:T(1024)(128)(4,1)}), s8[2097152]{0:T(1024)(128)(4,1)S(1)}, s32[]{:S(2)}) async-start(s8[6291456]{0:T(1024)(128)(4,1)} %bitcast.74), calls=%async_computation.9 | async-start | bytes 4194304 | tf_op jit(solution)/shard_map/while
  258.2 4.3 copy-start.2
  258.2 5.2 copy-start.4
  277.5 6.3 %copy-start.3 = (f32[4,512,1024]{2,1,0:T(8,128)S(1)}, f32[4,512,1024]{2,1,0:T(8,128)}, u32[]{:S(2)}) copy-start(f32[4,512,1024]{2,1,0:T(8,128)} %copy-done.2) | copy-start | bytes 25165828 | tf_op jit(solution)/shard_map/while
  277.5 6.8 %copy-start.11 = (bf16[2048,4,128]{2,0,1:T(8,128)(2,1)S(1)}, bf16[2048,4,128]{2,0,1:T(8,128)(2,1)}, u32[]{:S(2)}) copy-start(bf16[2048,4,128]{2,0,1:T(8,128)(2,1)} %get-tuple-element.355) | copy-start | bytes 6291460 | tf_op jit(solution)/shard_map/while
  277.5 13.4 %slice-start = ((s8[6291456]{0:T(1024)(128)(4,1)}), s8[4194304]{0:T(1024)(128)(4,1)S(1)}, s32[]{:S(2)}) async-start(s8[6291456]{0:T(1024)(128)(4,1)} %bitcast.74), calls=%async_computation.8 | async-start | bytes 8388608 | tf_op jit(solution)/shard_map/while
  284.3 6.5 %slice-start.1 = ((s8[6291456]{0:T(1024)(128)(4,1)}), s8[2097152]{0:T(1024)(128)(4,1)S(1)}, s32[]{:S(2)}) async-start(s8[6291456]{0:T(1024)(128)(4,1)} %bitcast.74), calls=%async_computation.9 | async-start | bytes 4194304 | tf_op jit(solution)/shard_map/while
  321.3 4.3 copy-start.2
  321.3 5.2 copy-start.4
  340.4 6.3 %copy-start.3 = (f32[4,512,1024]{2,1,0:T(8,128)S(1)}, f32[4,512,1024]{2,1,0:T(8,128)}, u32[]{:S(2)}) copy-start(f32[4,512,1024]{2,1,0:T(8,128)} %copy-done.2) | copy-start | bytes 25165828 | tf_op jit(solution)/shard_map/while
  340.4 6.8 %copy-start.11 = (bf16[2048,4,128]{2,0,1:T(8,128)(2,1)S(1)}, bf16[2048,4,128]{2,0,1:T(8,128)(2,1)}, u32[]{:S(2)}) copy-start(bf16[2048,4,128]{2,0,1:T(8,128)(2,1)} %get-tuple-element.355) | copy-start | bytes 6291460 | tf_op jit(solution)/shard_map/while
  340.4 13.3 %slice-start = ((s8[6291456]{0:T(1024)(128)(4,1)}), s8[4194304]{0:T(1024)(128)(4,1)S(1)}, s32[]{:S(2)}) async-start(s8[6291456]{0:T(1024)(128)(4,1)} %bitcast.74), calls=%async_computation.8 | async-start | bytes 8388608 | tf_op jit(solution)/shard_map/while
  347.2 6.5 %slice-start.1 = ((s8[6291456]{0:T(1024)(128)(4,1)}), s8[2097152]{0:T(1024)(128)(4,1)S(1)}, s32[]{:S(2)}) async-start(s8[6291456]{0:T(1024)(128)(4,1)} %bitcast.74), calls=%async_computation.9 | async-start | bytes 4194304 | tf_op jit(solution)/shard_map/while
  384.0 5.2 copy-start.4
  402.4 6.3 %copy-start.3 = (f32[4,512,1024]{2,1,0:T(8,128)S(1)}, f32[4,512,1024]{2,1,0:T(8,128)}, u32[]{:S(2)}) copy-start(f32[4,512,1024]{2,1,0:T(8,128)} %copy-done.2) | copy-start | bytes 25165828 | tf_op jit(solution)/shard_map/while
  402.4 6.8 %copy-start.11 = (bf16[2048,4,128]{2,0,1:T(8,128)(2,1)S(1)}, bf16[2048,4,128]{2,0,1:T(8,128)(2,1)}, u32[]{:S(2)}) copy-start(bf16[2048,4,128]{2,0,1:T(8,128)(2,1)} %get-tuple-element.355) | copy-start | bytes 6291460 | tf_op jit(solution)/shard_map/while
  402.4 13.3 %slice-start = ((s8[6291456]{0:T(1024)(128)(4,1)}), s8[4194304]{0:T(1024)(128)(4,1)S(1)}, s32[]{:S(2)}) async-start(s8[6291456]{0:T(1024)(128)(4,1)} %bitcast.74), calls=%async_computation.8 | async-start | bytes 8388608 | tf_op jit(solution)/shard_map/while
  409.3 6.5 %slice-start.1 = ((s8[6291456]{0:T(1024)(128)(4,1)}), s8[2097152]{0:T(1024)(128)(4,1)S(1)}, s32[]{:S(2)}) async-start(s8[6291456]{0:T(1024)(128)(4,1)} %bitcast.74), calls=%async_computation.9 | async-start | bytes 4194304 | tf_op jit(solution)/shard_map/while
  447.1 100.9 %all-to-all-start.2 = ((bf16[2048,4,192]{2,1,0:T(4,128)(2,1)}), bf16[2048,4,192]{2,1,0:T(4,128)(2,1)}, u32[]{:S(2)}, u32[]{:S(2)}) async-start(bf16[2048,4,192]{2,1,0:T(4,128)(2,1)} %copy.35), calls=%async_computation.2 | async-start | bytes 8388608 | tf_op jit(solution)/shard_map/all_to_all | solution.py:110
  453.0 87.4 %reduce-scatter.7.cloned.1.call-start = ((), (), s32[]{:S(2)}) async-start(), calls=%async_computation.7 | async-start | bytes 557056
  453.1 9.8 %copy-start.9 = (bf16[512,4,128]{0,2,1:T(8,128)(2,1)S(1)}, bf16[512,4,128]{0,2,1:T(8,128)(2,1)}, u32[]{:S(2)}) copy-start(bf16[512,4,128]{0,2,1:T(8,128)(2,1)} %copy-done.8) | copy-start | bytes 1572868
  462.9 142.5 %reduce-scatter.5.cloned.1.call-start = ((), (), s32[]{:S(2)}) async-start(), calls=%async_computation.6 | async-start | bytes 2228224 | tf_op jit(solution)/shard_map/reduce_scatter | solution.py:116
  (8 other events, 20.3 us)
Sparse Core Ops, SparseCore 0:
  71.9 64.2 all-gather.1
  463.0 77.3 reduce-scatter.6
  545.2 60.1 reduce-scatter.4
where the time goes:
time: 622 us; the launch traced here: 612 us
  local copies, waits for them, and re-layouts  179 us (29%)
  blocking collectives  142 us (23%)
  matrix products  131 us (21%)
  waiting for transfers between devices  115 us (18%)
  other arithmetic  17 us (3%)
  between operations  13.9 us (2%)
  starting transfers between devices  12.1 us (2%)
    all_gather x1, blocking collectives, shards(): lax.all_gather(rope_key, 'head', axis=0, tiled=True)  89.8 us
    dynamic_update_slice x4, local copies, waits for them, and re-layouts, backward_block(): lax.dynamic_update_slice_in_dim(key_grad, lax.dynamic_slice_in_dim(key_gr...  61.6 us
    unnamed x4, waiting for transfers between devices  59.1 us
    all_to_all x1, blocking collectives, shards(): lax.all_to_all(out_grad, 'head', split_axis=1, concat_axis=0, tiled=True)  52.7 us
    reduce_scatter x1, waiting for transfers between devices, shards(): lax.psum_scatter(latent_part.astype(jnp.bfloat16), 'head', scatter_dimens...  50.2 us
    dynamic_update_slice x4, local copies, waits for them, and re-layouts, backward_block(): lax.dynamic_update_slice_in_dim(value_grad, lax.dynamic_slice_in_dim(valu...  40.3 us
    dot_general x4, matrix products, backward_block(): jnp.einsum('hij,jhd->ihd', probs_low, value_block, preferred_element_type...  25.1 us
    while x56, local copies, waits for them, and re-layouts  21.2 us
  transfers between devices with their start and end apart: 5, of which 3 were waited for; matrix products, arithmetic and copies ran while one was open for 8% of the time, Pallas kernels for 0%

commit v1 on v0

v1 whole, which is shorter than its diff:
```python
import functools
import math

import jax
import jax.numpy as jnp
from jax import lax
from jax.experimental import pallas as pl
from jax.experimental.pallas import tpu as pltpu
from jax.sharding import PartitionSpec as P

WIDE = jnp.float32
LOW = jnp.bfloat16
MESH = pl.DeviceIdType.MESH
NT = (((1,), (1,)), ((), ()))


def dot(a, b):
    return jnp.dot(a, b, preferred_element_type=WIDE)


def dot_nt(a, b):
    return lax.dot_general(a, b, NT, preferred_element_type=WIDE)


def kernel(
    n, scale,
    x_ref, l_ref, w_ref, fk_ref,
    y_ref, g_ref, ku_ref, vu_ref,
    xr, la, lat, kk, kt, vv, kg, vg, lp, rp, ys, ls, lr,
    sx, rx, sl, rl, sy, ry, sg, rg, lsem, osem,
):
    me = lax.axis_index("head")
    pairs, rows, lanes = x_ref.shape[1], x_ref.shape[3], x_ref.shape[4]
    width = l_ref.shape[1] - lanes
    seq = n * rows
    block = 2 * rows
    reach = 4 * rows
    window = block + reach
    half = lanes // 2

    def peers(body):
        def step(k, _):
            body(lax.rem(me + k, n))
            return 0

        lax.fori_loop(1, n, step, 0)

    def remote(src, dst, send, recv, peer):
        return pltpu.make_async_remote_copy(
            src_ref=src, dst_ref=dst, send_sem=send, recv_sem=recv,
            device_id={"head": peer}, device_id_type=MESH,
        )

    def copy_l(src_dev, peer):
        return remote(l_ref, la.at[pl.ds(src_dev * rows, rows)],
                      sl.at[peer], rl.at[src_dev], peer)

    spans = (pl.ds(0, 3), pl.ds(3, 2))

    def copy_x(pair, odd, src_dev, peer):
        return remote(x_ref.at[peer, pair, spans[odd]], xr.at[src_dev, pair, spans[odd]],
                      sx.at[2 * pair + odd, peer], rx.at[2 * pair + odd, src_dev], peer)

    outs = (pl.ds(0, 1), pl.ds(1, 2))

    def copy_y(pair, odd, src_dev, peer):
        return remote(ys.at[peer, pair, outs[odd]], y_ref.at[src_dev, pair, outs[odd]],
                      sy.at[2 * pair + odd, peer], ry.at[2 * pair + odd, src_dev], peer)

    def copy_g(src_dev, peer):
        return remote(ls.at[pl.ds(peer * rows, rows)], lr.at[src_dev],
                      sg.at[peer], rg.at[src_dev], peer)

    own_l = pltpu.make_async_copy(l_ref, la.at[pl.ds(me * rows, rows)], lsem.at[0])
    own_x = pltpu.make_async_copy(x_ref.at[me], xr.at[me], lsem.at[1])
    own_l.start()
    own_x.start()

    barrier = pltpu.get_barrier_semaphore()
    peers(lambda p: pl.semaphore_signal(
        barrier, inc=1, device_id={"head": p}, device_id_type=MESH))
    pl.semaphore_wait(barrier, n - 1)

    peers(lambda p: copy_l(me, p).start())

    def send_pair(pair, _):
        for odd in range(2):
            peers(lambda p: copy_x(pair, odd, me, p).start())
        return 0

    lax.fori_loop(0, pairs, send_pair, 0)

    kk[pl.ds(0, reach), :] = jnp.zeros((reach, 2 * lanes), LOW)
    kt[:, pl.ds(0, reach)] = jnp.zeros((2 * lanes, reach), LOW)
    vv[pl.ds(0, reach), :] = jnp.zeros((reach, lanes), LOW)
    low_half = lax.broadcasted_iota(jnp.int32, (block, lanes), 1) < half

    own_l.wait()
    peers(lambda p: copy_l(p, p).wait_recv())
    own_x.wait()

    def flip(t, _):
        at = pl.ds(pl.multiple_of(t * block, block), block)
        lat[:, at] = la[at, pl.ds(0, width)].T
        rp[at, :] = jnp.zeros((block, lanes), WIDE)
        lp[at, :] = jnp.zeros((block, width), WIDE)
        return 0

    lax.fori_loop(0, seq // block, flip, 0)

    def clear(t, _):
        at = pl.ds(pl.multiple_of(t * block, block), block)
        kg[at, :] = jnp.zeros((block, 2 * lanes), WIDE)
        vg[at, :] = jnp.zeros((block, lanes), WIDE)
        return 0

    def one_head(pair, odd):
        head = 2 * pair + odd
        keep = jnp.logical_not(low_half) if odd else low_half
        zero_low = jnp.zeros((block, lanes), WIDE)

        def expand(t, _):
            at = pl.ds(pl.multiple_of(t * block, block), block)
            to = pl.ds(pl.multiple_of(t * block + reach, block), block)
            both = dot(la[at, pl.ds(0, width)], w_ref[head])
            rope = jnp.where(keep, la[at, pl.ds(width, lanes)].astype(WIDE), zero_low)
            keys = jnp.concatenate([both[:, :lanes], rope], axis=1)
            kk[to, :] = keys.astype(LOW)
            kt[:, to] = keys.T.astype(LOW)
            vv[to, :] = both[:, lanes:].astype(LOW)
            return 0

        lax.fori_loop(0, seq // block, expand, 0)
        lax.fori_loop(0, (seq + reach) // block, clear, 0)
        peers(lambda p: copy_x(pair, odd, p, p).wait_recv())

        def attend(b, _):
            start = pl.multiple_of(b * block, block)
            win = pl.ds(start, window)
            src = pl.ds(2 * b, 2)
            nope = xr[src, pair, 1 + 2 * odd].reshape(block, lanes)
            grad = xr[src, pair, 2 + 2 * odd].reshape(block, lanes)
            rope = xr[src, pair, 0].reshape(block, lanes)
            q = jnp.concatenate([nope, rope], axis=1)
            s = dot_nt(kk[win, :], q)
            pg = dot_nt(vv[win, :], grad)
            col = lax.broadcasted_iota(jnp.int32, (window, block), 0) + (start - reach)
            row = lax.broadcasted_iota(jnp.int32, (1, block), 1) + start
            first = fk_ref[:, pl.ds(start, block)]
            s = jnp.where((col >= first) & (col <= row), s, -jnp.inf)
            peak = jnp.max(s, axis=0, keepdims=True)
            e = jnp.exp2((s - peak) * (scale * math.log2(math.e)))
            inv = 1.0 / jnp.sum(e, axis=0, keepdims=True)
            delta = jnp.sum(e * pg, axis=0, keepdims=True) * inv
            p = e * inv
            ds = (p * (pg - delta)).astype(LOW)
            vg[win, :] += dot(p.astype(LOW), grad)
            kg[win, :] += dot(ds, q)
            qg = (dot(kt[:, win], ds) * scale).T.astype(LOW)
            ys[src, pair, odd] = qg[:, :lanes].reshape(2, rows, lanes)
            if odd:
                other = ys[src, pair, 2].reshape(block, lanes)
                rope_out = jnp.where(low_half, other.astype(WIDE), qg[:, lanes:].astype(WIDE))
                ys[src, pair, 2] = rope_out.astype(LOW).reshape(2, rows, lanes)
            else:
                ys[src, pair, 2] = qg[:, lanes:].reshape(2, rows, lanes)
            return 0

        lax.fori_loop(0, n // 2, attend, 0)
        peers(lambda p: copy_y(pair, odd, me, p).start())

        def finish(t, carry):
            ku, vu = carry
            at = pl.ds(pl.multiple_of(t * block, block), block)
            frm = pl.ds(pl.multiple_of(t * block + reach, block), block)
            keys = kg[frm, :] * scale
            low = jnp.concatenate([keys[:, :lanes].astype(LOW), vg[frm, :].astype(LOW)], axis=1)
            rope = keys[:, lanes:].astype(LOW).astype(WIDE)
            rp[at, :] += jnp.where(keep, rope, zero_low)
            lp[at, :] += dot_nt(low, w_ref[head])
            up = dot(lat[:, at], low)
            return ku + up[:, :lanes], vu + up[:, lanes:]

        zero = jnp.zeros((width, lanes), WIDE)
        ku, vu = lax.fori_loop(0, seq // block, finish, (zero, zero))
        ku_ref[head] = ku
        vu_ref[head] = vu

    def both_heads(pair, _):
        one_head(pair, 0)
        one_head(pair, 1)
        return 0

    lax.fori_loop(0, pairs, both_heads, 0)
    own_y = pltpu.make_async_copy(ys.at[me], y_ref.at[me], osem)
    own_y.start()

    def pack(t, _):
        at = pl.ds(pl.multiple_of(t * block, block), block)
        ls[at, pl.ds(0, width)] = lp[at, :].astype(LOW)
        ls[at, pl.ds(width, lanes)] = rp[at, :].astype(LOW)
        return 0

    lax.fori_loop(0, seq // block, pack, 0)
    peers(lambda p: copy_g(me, p).start())

    def add(k, total):
        p = lax.rem(me + k, n)
        copy_g(p, p).wait_recv()
        return total + lr[p].astype(WIDE)

    total = ls[pl.ds(me * rows, rows), :].astype(WIDE)
    g_ref[...] = lax.fori_loop(1, n, add, total)

    own_y.wait()
    peers(lambda p: copy_l(me, p).wait_send())
    peers(lambda p: copy_g(me, p).wait_send())

    def drain(pair, _):
        for odd in range(2):
            peers(lambda p: copy_x(pair, odd, me, p).wait_send())
            peers(lambda p: copy_y(pair, odd, me, p).wait_send())
            peers(lambda p: copy_y(pair, odd, p, p).wait_recv())
        return 0

    lax.fori_loop(0, pairs, drain, 0)


def shards(queries, latent, rope_key, key_up, value_up, first_key, out_grad):
    n = lax.axis_size("head")
    rows, all_heads, qk = queries.shape
    width, heads, nope = key_up.shape
    rope = qk - nope
    lanes = out_grad.shape[2]
    pairs = heads // 2
    seq = rows * n
    reach = 4 * rows
    scale = 1.0 / math.sqrt(qk)

    q = queries.reshape(rows, n, pairs, 2, qk)
    d = out_grad.reshape(rows, n, pairs, 2, lanes)
    q_rope = q[..., nope:].reshape(rows, n, pairs, 2 * rope)
    x = jnp.stack(
        [q_rope, q[:, :, :, 0, :nope], d[:, :, :, 0], q[:, :, :, 1, :nope], d[:, :, :, 1]],
        axis=3,
    ).transpose(1, 2, 3, 0, 4)
    lcat = jnp.concatenate([latent, rope_key, rope_key], axis=1)
    w = jnp.concatenate([key_up, value_up], axis=2).transpose(1, 0, 2)

    any_spec = pl.BlockSpec(memory_space=pl.ANY)
    vmem = pl.BlockSpec(memory_space=pltpu.VMEM)
    dma = pltpu.SemaphoreType.DMA
    total_w = width + lanes
    y, g, ku, vu = pl.pallas_call(
        functools.partial(kernel, n, scale),
        out_shape=[
            jax.ShapeDtypeStruct((n, pairs, 3, rows, lanes), LOW),
            jax.ShapeDtypeStruct((rows, total_w), WIDE),
            jax.ShapeDtypeStruct((heads, width, lanes), WIDE),
            jax.ShapeDtypeStruct((heads, width, lanes), WIDE),
        ],
        in_specs=[any_spec, any_spec, vmem, vmem],
        out_specs=[any_spec, vmem, vmem, vmem],
        scratch_shapes=[
            pltpu.VMEM((n, pairs, 5, rows, lanes), LOW),
            pltpu.VMEM((seq, total_w), LOW),
            pltpu.VMEM((width, seq), LOW),
            pltpu.VMEM((reach + seq, 2 * lanes), LOW),
            pltpu.VMEM((2 * lanes, reach + seq), LOW),
            pltpu.VMEM((reach + seq, lanes), LOW),
            pltpu.VMEM((reach + seq, 2 * lanes), WIDE),
            pltpu.VMEM((reach + seq, lanes), WIDE),
            pltpu.VMEM((seq, width), WIDE),
            pltpu.VMEM((seq, lanes), WIDE),
            pltpu.VMEM((n, pairs, 3, rows, lanes), LOW),
            pltpu.VMEM((seq, total_w), LOW),
            pltpu.VMEM((n, rows, total_w), LOW),
            dma((heads, n)), dma((heads, n)),
            dma((n,)), dma((n,)),
            dma((heads, n)), dma((heads, n)),
            dma((n,)), dma((n,)),
            dma((2,)), dma,
        ],
        compiler_params=pltpu.CompilerParams(
            collective_id=0, has_side_effects=True, vmem_limit_bytes=62 * 1024 * 1024
        ),
    )(x, lcat, w, first_key.reshape(1, seq))

    y_nope = y[:, :, :2].transpose(3, 0, 1, 2, 4)
    y_rope = y[:, :, 2].transpose(2, 0, 1, 3).reshape(rows, n, pairs, 2, rope)
    query_out = jnp.concatenate([y_nope, y_rope], axis=4).reshape(rows, all_heads, qk)
    latent_grad = g[:, :width].astype(LOW)
    rope_grad = (g[:, width : width + rope] + g[:, width + rope :]).astype(LOW)
    return (query_out, latent_grad, rope_grad, ku.transpose(1, 0, 2), vu.transpose(1, 0, 2))


def solution(mesh):
    return jax.shard_map(
        shards,
        mesh=mesh,
        in_specs=(
            P(("group", "head"), None, None),
            P(("group", "head"), None),
            P(("group", "head"), None),
            P(None, "head", None),
            P(None, "head", None),
            P("group"),
            P(("group", "head"), None, None),
        ),
        out_specs=(
            P(("group", "head"), None, None),
            P(("group", "head"), None),
            P(("group", "head"), None),
            P("group", "head", None),
            P("group", "head", None),
        ),
        check_vma=False,
    )
```

time: 622 us -> 347 us (0.56); the launches traced: 612 us -> 346 us
  Pallas kernels: 0 us -> 308 us
  local copies, waits for them, and re-layouts: 179 us -> 31.7 us
  blocking collectives: 142 us -> 0 us
  matrix products: 131 us -> 0 us
  waiting for transfers between devices: 115 us -> 0 us
  between operations: 13.9 us -> 0.81 us
  starting transfers between devices: 12.1 us -> 0 us
  other arithmetic: 17 us -> 5.16 us
    pallas_call x0 -> x1, Pallas kernels: none -> 308 us  [shards(): pl.pallas_call(functools.partial(kernel, n, scale), out_shape=[jax.ShapeD...]
    dot_general x29 -> x0, matrix products: 129 us -> none  [the longest x4 25.1 us: backward_block(): jnp.einsum('hij,jhd->ihd', probs_low, value_block, preferred_element_type...]
    dynamic_update_slice x8 -> x0, local copies, waits for them, and re-layouts: 102 us -> none  [the longest x4 61.6 us: backward_block(): lax.dynamic_update_slice_in_dim(key_grad, lax.dynamic_slice_in_dim(key_gr...]
    all_gather x1 -> x0, blocking collectives: 89.8 us -> none  [shards(): lax.all_gather(rope_key, 'head', axis=0, tiled=True)]
    unnamed x4 -> x0, waiting for transfers between devices: 59.1 us -> none
    all_to_all x1 -> x0, blocking collectives: 52.7 us -> none  [shards(): lax.all_to_all(out_grad, 'head', split_axis=1, concat_axis=0, tiled=True)]
    reduce_scatter x1 -> x0, waiting for transfers between devices: 50.2 us -> none  [shards(): lax.psum_scatter(latent_part.astype(jnp.bfloat16), 'head', scatter_dimens...]
    while x58 -> x0, local copies, waits for them, and re-layouts: 35.1 us -> none
  transfers between devices with their start and end apart: 5 -> 0, of which waited for: 3 -> 0; matrix products, arithmetic and copies ran while one was open for 8% -> 0% of each run, Pallas kernels for 0% -> 0%
where the time goes in v1:
time: 347 us; the launch traced here: 346 us
  Pallas kernels  308 us (89%)
  local copies, waits for them, and re-layouts  31.7 us (9%)
  other arithmetic  5.16 us (1%)
    pallas_call x1, Pallas kernels, shards(): pl.pallas_call(functools.partial(kernel, n, scale), out_shape=[jax.ShapeD...  308 us
    unnamed x28, local copies, waits for them, and re-layouts  18.6 us

profile of v1, /device:TPU:31, one launch (start us, length us, event | category | flops | bytes accessed | tf_op | source)
XLA Modules:
  0.0 346.0 jit_solution(3464703333215490296)
XLA Ops:
  0.6 5.9 %copy.22 = bf16[128,64,192]{2,0,1:T(8,128)(2,1)} copy(bf16[128,64,192]{0,2,1:T(8,128)(2,1)} %param.7) | data formatting | bytes 6291456 | tf_op args[0]
  6.5 1.7 slice.41
  8.3 0.9 copy.23
  9.2 0.7 copy.25
  9.9 0.0 copy-start.1
  9.9 0.1 constant_dynamic-update-slice_fusion
  10.0 1.5 slice_dynamic-update-slice_fusion.3
  11.5 0.3 copy-done.1
  11.8 1.4 copy.24
  13.1 0.0 copy-start.3
  13.2 0.0 copy-start.4
  13.2 0.1 slice_dynamic-update-slice_fusion.2
  13.3 0.0 copy-start.7
  13.3 1.5 slice_dynamic-update-slice_fusion.1
  14.9 0.1 slice_dynamic-update-slice_fusion
  15.0 2.3 copy-done
  17.3 0.1 copy.28
  17.4 0.1 copy.29
  17.5 1.1 maximum_bitcast_fusion.w_ref
  18.6 0.1 copy.26
  18.7 0.8 pad_maximum_fusion.1.l_ref
  19.4 308.4 %shard_map.110 = (bf16[16,2,3,128,128]{4,3,2,1,0:T(8,128)(2,1)}, f32[128,640]{1,0:T(8,128)}, f32[4,512,128]{2,1,0:T(8,128)}, f32[4,512,128]{2,1,0:T(8,128)}) custom-call(bf16[16,2,5,128,128]{4,3,2,1,0:T(8,128)(2,1)} %bitcast.23, bf16[128,640]{1,0:T(8,128)(2,1)} %pad_maximum_fusion.1.l_ref, bf16[4,512,256]{2,1,0:T(8,128)(2,1)} %maximum_bitcast_fusion.w_ref, ...), custom_call_target="tpu_custom_call" | custom-call | tf_op jit(solution)/shard_map/pallas_call | solution.py:254
  327.8 3.2 slice.36
  331.0 3.2 copy.31
  334.2 1.3 slice_bitcast_fusion
  335.5 1.3 copy.30
  336.8 3.2 pad_maximum_fusion
  340.1 0.7 slice.55
  340.7 0.1 add_convert_fusion
  340.8 0.7 copy.32
  341.5 2.9 copy.33
  344.4 1.6 copy.34
  (10 shorter events, 0.0 us)
Async XLA Ops:
  9.9 1.9 copy-start.1
  13.1 4.2 %copy-start.3 = (bf16[512,4,128]{2,1,0:T(4,128)(2,1)S(1)}, bf16[512,4,128]{2,1,0:T(4,128)(2,1)}, u32[]{:S(2)}) copy-start(bf16[512,4,128]{2,1,0:T(4,128)(2,1)} %param.10) | copy-start | bytes 1572868
  13.2 4.2 %copy-start.4 = (bf16[512,4,128]{2,1,0:T(4,128)(2,1)S(1)}, bf16[512,4,128]{2,1,0:T(4,128)(2,1)}, u32[]{:S(2)}) copy-start(bf16[512,4,128]{2,1,0:T(4,128)(2,1)} %param.11) | copy-start | bytes 1572868
  13.3 5.2 %copy-start.7 = (bf16[128,64]{0,1:T(8,128)(2,1)S(1)}, bf16[128,64]{0,1:T(8,128)(2,1)}, u32[]{:S(2)}) copy-start(bf16[128,64]{0,1:T(8,128)(2,1)} %param.9) | copy-start | bytes 49156
  13.3 5.3 %copy-start.6 = (bf16[128,512]{1,0:T(8,128)(2,1)S(1)}, bf16[128,512]{1,0:T(8,128)(2,1)}, u32[]{:S(2)}) copy-start(bf16[128,512]{1,0:T(8,128)(2,1)} %param.8) | copy-start | bytes 393220
  15.0 2.3 copy-start
  335.5 4.6 %copy-start.5 = (f32[128,640]{1,0:T(8,128)S(1)}, f32[128,640]{1,0:T(8,128)}, u32[]{:S(2)}) copy-start(f32[128,640]{1,0:T(8,128)} %get-tuple-element.10) | copy-start | bytes 983044
  336.8 7.6 %copy-start.2 = (f32[4,512,128]{2,1,0:T(8,128)S(1)}, f32[4,512,128]{2,1,0:T(8,128)}, u32[]{:S(2)}) copy-start(f32[4,512,128]{2,1,0:T(8,128)} %get-tuple-element.12) | copy-start | bytes 3145732
